TPU v7x, 32 devices: a whole 2x2x4 slice. The times are simulated.
32 devices in a mesh: group: 2 (over x), expert: 8 (over z, y), dp: 2 (over core).
Axes of the slice: x: 2, y: 2, z: 4, core: 2. Of those that a mesh axis runs over, the one named last changes fastest.
Arguments:
- tokens: bfloat16 [4096, 4096], P(('group', 'expert', 'dp')), parts along dimension 0, may hold values from -6 to 6
- out_grad: bfloat16 [4096, 4096], P(('group', 'expert', 'dp')), parts along dimension 0, may hold values from -6 to 6
- routes: int32 [4096, 2], P('group'), parts along dimension 0, may hold values from 0 to 3, all different within a row
- route_weight: float32 [4096, 2], P('group'), parts along dimension 0, may hold values from 0.1 to 0.9
- gate_pre: bfloat16 [8, 1536, 3584], P('expert', ('group', 'dp')), parts along dimension 1, may hold values from -6 to 6
- up_pre: bfloat16 [8, 1536, 3584], P('expert', ('group', 'dp')), parts along dimension 1, may hold values from -6 to 6
- hid_grad: bfloat16 [8, 1536, 3584], P('expert', ('group', 'dp')), parts along dimension 1, may hold values from -6 to 6
- proj_model: bfloat16 [4096, 64], replicated, may hold values from -0.09375 to 0.09375
- proj_hidden: bfloat16 [7168, 64], replicated, may hold values from -0.0625 to 0.0625
- val_sketch: bfloat16 [128, 49152], P('dp', 'expert'), may hold values from -0.00390625 to 0.00390625
Outputs:
- influence: float32 [4, 128], P('group', 'dp'), parts along dimension 0
There are 2 independent parts, one for each index of `group`. A program takes and returns all parts, laid end to end along the dimension named above; an argument that names none is the same for every part. Nothing has to cross between parts.
Inputs may be any that keep to these rules, and one draw needn't show every extreme that they name: `routes`: the two experts of a row differ; every expert is named by some row.
All inputs are finite; a program needn't handle non-finite values.
Results may differ from a plain program's by a relative error of at most 0.0055.
Values may be sent and summed in bfloat16 or wider, within the bound.
A program may use at most 128 MiB of HBM per device.

v0:
```python
import jax
import jax.numpy as jnp
from jax import lax
from jax.sharding import PartitionSpec as P

HALVES = 2
EX_DP = 1


def partner_2(value, axis, stride):
    mask = 2**stride
    pairs = [(source, source ^ mask) for source in range(lax.axis_size(axis))]
    return lax.ppermute(value, axis, pairs)


def slot_ranks(block_routes, experts):
    labels = jnp.arange(experts, dtype=jnp.int32)
    onehot = (block_routes[..., None] == labels).astype(jnp.int32)
    before = jnp.cumsum(onehot, axis=-2) - onehot
    return jnp.sum(before * onehot, axis=-1)


def swiglu_back(gate_pre, up_pre, hid_grad):
    gate_vals = gate_pre.astype(jnp.float32)
    up_vals = up_pre.astype(jnp.float32)
    grad_vals = hid_grad.astype(jnp.float32)
    gate_sig = jax.nn.sigmoid(gate_vals)
    silu_vals = gate_vals * gate_sig
    hidden = (silu_vals * up_vals).astype(jnp.bfloat16)
    grad_gate = (grad_vals * up_vals * gate_sig * (1.0 + gate_vals * (1.0 - gate_sig))).astype(
        jnp.bfloat16
    )
    grad_up = (grad_vals * silu_vals).astype(jnp.bfloat16)
    return (hidden, grad_gate, grad_up)


def shards(
    tokens,
    out_grad,
    routes,
    route_weight,
    gate_pre,
    up_pre,
    hid_grad,
    proj_model,
    proj_hidden,
    val_sketch,
):
    expert_count = lax.axis_size("expert")
    dp_count = lax.axis_size("dp")
    here_expert = lax.axis_index("expert")
    here_dp = lax.axis_index("dp")
    experts = expert_count // HALVES
    tok_rows = tokens.shape[0]
    pair_count = 2 * tok_rows
    slot_rows = gate_pre.shape[1]
    capacity = slot_rows // expert_count
    seq_rows = tok_rows // EX_DP
    route_grid = routes.reshape(expert_count, dp_count, pair_count)
    weight_grid = route_weight.reshape(expert_count, dp_count, pair_count)
    expert_ids = jnp.arange(experts, dtype=jnp.int32)
    slot_ids = jnp.arange(capacity, dtype=jnp.int32)
    own_routes = route_grid[here_expert, here_dp]
    own_ranks = slot_ranks(own_routes, experts)
    chosen = (
        (own_routes[None, None, :] == expert_ids[:, None, None])
        & (own_ranks[None, None, :] == slot_ids[None, :, None])
    ).astype(jnp.bfloat16)
    own_expert = here_expert // HALVES
    column_half = here_expert % HALVES
    source_routes = route_grid[:, here_dp]
    source_ranks = slot_ranks(source_routes, experts)
    matched = (
        (source_routes == own_expert)[:, None, :]
        & (source_ranks[:, None, :] == slot_ids[None, :, None])
    ).astype(jnp.int32)
    pair_index = jnp.sum(matched * jnp.arange(pair_count, dtype=jnp.int32), axis=-1).reshape(-1)
    filled = jnp.sum(matched, axis=-1).reshape(-1)
    example = pair_index // 2 // seq_rows
    member = (
        (example[:, None] == jnp.arange(EX_DP, dtype=jnp.int32)[None, :]) & (filled[:, None] > 0)
    ).astype(jnp.bfloat16)
    chosen_rows = jnp.sum(chosen.reshape(experts, capacity, tok_rows, 2), axis=3)
    buffer_tokens = jnp.einsum(
        "ejt,tw->ejw", chosen_rows, tokens, preferred_element_type=jnp.float32
    ).astype(jnp.bfloat16)
    buffer_grads = jnp.einsum(
        "ejt,tw->ejw", chosen_rows, out_grad, preferred_element_type=jnp.float32
    ).astype(jnp.bfloat16)
    recv_tokens, recv_grads = (
        lax.all_to_all(
            jnp.repeat(buffer_tokens, HALVES, axis=0),
            "expert",
            split_axis=0,
            concat_axis=0,
            tiled=True,
        ),
        lax.all_to_all(
            jnp.repeat(buffer_grads, HALVES, axis=0),
            "expert",
            split_axis=0,
            concat_axis=0,
            tiled=True,
        ),
    )
    slot_weight = jnp.sum(
        matched.astype(jnp.float32) * weight_grid[:, here_dp][:, None, :], axis=-1
    ).reshape(-1)
    slot_inputs = jnp.dot(
        recv_tokens.reshape(slot_rows, -1), proj_model, preferred_element_type=jnp.float32
    ).astype(jnp.bfloat16)
    grads_rows = jnp.dot(
        recv_grads.reshape(slot_rows, -1), proj_model, preferred_element_type=jnp.float32
    )
    slot_grads = (slot_weight[:, None] * grads_rows).astype(jnp.bfloat16)
    hidden, grad_gate, grad_up = swiglu_back(gate_pre[0], up_pre[0], hid_grad[0])
    column_width = gate_pre.shape[2]
    factor = lax.dynamic_slice_in_dim(proj_hidden, column_half * column_width, column_width, 0)
    blocks = []
    for values, partner in ((hidden, slot_grads), (grad_gate, slot_inputs), (grad_up, slot_inputs)):
        projected = jnp.dot(values, factor, preferred_element_type=jnp.float32).astype(jnp.bfloat16)
        weighted = member[:, :, None] * partner[:, None, :]
        blocks.append(
            jnp.einsum("ra,rib->iab", projected, weighted, preferred_element_type=jnp.float32)
        )
    partial_value = jnp.stack(blocks, axis=1).reshape(EX_DP, -1)
    half_len = partial_value.shape[1] // HALVES
    kept_half = lax.dynamic_slice_in_dim(partial_value, column_half * half_len, half_len, 1)
    sent_half = lax.dynamic_slice_in_dim(partial_value, (1 - column_half) * half_len, half_len, 1)
    sketch = (kept_half + partner_2(sent_half, "expert", 0)).astype(jnp.bfloat16)
    scores = lax.dot_general(
        lax.all_gather(sketch, "dp", axis=0, tiled=True),
        val_sketch,
        (((1,), (1,)), ((), ())),
        preferred_element_type=jnp.float32,
    )
    return lax.psum(scores, "expert")


def solution(mesh):
    return jax.shard_map(
        shards,
        mesh=mesh,
        in_specs=(
            P(("group", "expert", "dp"), None),
            P(("group", "expert", "dp"), None),
            P("group", None),
            P("group", None),
            P("expert", ("group", "dp"), None),
            P("expert", ("group", "dp"), None),
            P("expert", ("group", "dp"), None),
            P(),
            P(),
            P("dp", "expert"),
        ),
        out_specs=P("group", "dp"),
        check_vma=False,
    )
```

profile of v0, /device:TPU:0, one launch (start us, length us, event | category | flops | bytes accessed | tf_op | source)
XLA Modules:
  0.0 192.2 jit_solution(16231146610534312536)
XLA Ops:
  0.0 1.2 copy.27
  1.2 0.6 reshape.186
  1.8 0.5 broadcast.205
  2.3 0.7 fusion.81
  3.0 1.2 reduce-window.16
  5.1 0.6 convolution_convert_fusion
  5.7 2.1 %broadcast_in_dim.5 = bf16[4,2,48,4096]{3,2,1,0:T(8,128)(2,1)} broadcast(bf16[4,48,4096]{2,1,0:T(8,128)(2,1)S(1)} %convolution_convert_fusion), dimensions={0,2,3} | broadcast | bytes 4718592 | tf_op jit(solution)/shard_map/broadcast_in_dim | solution.py:92
  7.8 7.3 %all-to-all-start.1 = ((bf16[8,48,4096]{2,1,0:T(8,128)(2,1)}), bf16[8,48,4096]{2,1,0:T(8,128)(2,1)}, u32[]{:S(2)}, u32[]{:S(2)}) async-start(bf16[8,48,4096]{2,1,0:T(8,128)(2,1)} %bitcast.159), calls=%async_computation.1 | async-start | bytes 6291456 | tf_op jit(solution)/shard_map/all_to_all | solution.py:91
  15.1 1.8 convolution_convert_fusion.1
  16.9 69.0 %all-to-all-done.1 = bf16[8,48,4096]{2,1,0:T(8,128)(2,1)} async-done(((bf16[8,48,4096]{2,1,0:T(8,128)(2,1)}), bf16[8,48,4096]{2,1,0:T(8,128)(2,1)}, u32[]{:S(2)}, u32[]{:S(2)}) %all-to-all-start.1) | async-done | bytes 3145760 | tf_op jit(solution)/shard_map/all_to_all | solution.py:91
  85.9 2.1 %broadcast_in_dim.4 = bf16[4,2,48,4096]{3,2,1,0:T(8,128)(2,1)} broadcast(bf16[4,48,4096]{2,1,0:T(8,128)(2,1)S(1)} %convolution_convert_fusion.1), dimensions={0,2,3} | broadcast | bytes 4718592 | tf_op jit(solution)/shard_map/broadcast_in_dim | solution.py:99
  88.0 4.8 %all-to-all-start = ((bf16[8,48,4096]{2,1,0:T(8,128)(2,1)}), bf16[8,48,4096]{2,1,0:T(8,128)(2,1)}, u32[]{:S(2)}, u32[]{:S(2)}) async-start(bf16[8,48,4096]{2,1,0:T(8,128)(2,1)} %bitcast.158), calls=%async_computation | async-start | bytes 6291456 | tf_op jit(solution)/shard_map/all_to_all | solution.py:98
  92.8 2.3 %reduce-window.14 = s32[8,4,2,128]{3,0,1,2:T(8,128)S(1)} reduce-window(s32[8,4,2,128]{3,0,1,2:T(8,128)S(1)} %fusion.58, s32[]{:T(128)} %constant.64.clone.1), window={size=1x1x1x128 pad=0_0x0_0x0_0x127_0}, to_apply=%region_0.0 | reduce-window | flops 1040384 | bytes 65540 | tf_op jit(solution)/shard_map/reduce-window
  96.4 0.6 reshape.189
  97.3 4.5 %fusion.21 = bf16[384,64]{0,1:T(8,128)(2,1)S(1)} fusion(bf16[1,384,3584]{2,1,0:T(8,128)(2,1)} %param.15, bf16[1,384,3584]{2,1,0:T(8,128)(2,1)} %param.14, bf16[7168,64]{0,1:T(8,128)(2,1)S(1)} %copy-done.3, s32[]{:T(128)S(6)} %select_n.52), kind=kOutput, calls=%fused_computation.26 | convolution fusion | flops 187195392 | bytes 6012932 | tf_op jit(solution)/shard_map/dot_general | solution.py:121
  101.8 3.0 %fusion.27 = bf16[384,64]{0,1:T(8,128)(2,1)S(1)} fusion(bf16[384,4096]{1,0:T(8,128)(2,1)} %bitcast.17, bf16[4096,64]{0,1:T(8,128)(2,1)S(1)} %copy-done.1, bf16[384]{0:T(512)(128)(2,1)S(1)} %and_convert_fusion.1), kind=kOutput, calls=%fused_computation.28 | convolution fusion | flops 201375744 | bytes 3719936 | tf_op jit(solution)/shard_map/dot_general | solution.py:109
  104.8 4.6 %fusion.39 = f32[1,1,64,64]{2,3,1,0:T(8,128)S(1)} fusion(bf16[384,64]{0,1:T(8,128)(2,1)S(1)} %fusion.27, bf16[1,384,3584]{2,1,0:T(8,128)(2,1)} %param.16, bf16[1,384,3584]{2,1,0:T(8,128)(2,1)} %param.14, bf16[7168,64]{0,1:T(8,128)(2,1)S(1)} %copy-done.3, s32[]{:T(128)S(6)} %select_n.52), kind=kOutput, calls=%fused_computation.34 | convolution fusion | flops 190341120 | bytes 6029316 | tf_op jit(solution)/shard_map/ra,rib->iab/dot_general | solution.py:124
  109.5 6.2 %fusion.36 = f32[1,1,64,64]{2,3,1,0:T(8,128)S(1)} fusion(bf16[384,64]{0,1:T(8,128)(2,1)S(1)} %fusion.27, bf16[1,384,3584]{2,1,0:T(8,128)(2,1)} %param.16, bf16[1,384,3584]{2,1,0:T(8,128)(2,1)} %param.15, bf16[1,384,3584]{2,1,0:T(8,128)(2,1)} %param.14, bf16[7168,64]{0,1:T(8,128)(2,1)S(1)} %copy-done.3, s32[]{:T(128)S(6)} %select_n.52), kind=kOutput, calls=%fused_computation.33 | convolution fusion | flops 197222400 | bytes 8781828 | tf_op jit(solution)/shard_map/ra,rib->iab/dot_general | solution.py:124
  115.7 47.1 %all-to-all-done = bf16[8,48,4096]{2,1,0:T(8,128)(2,1)} async-done(((bf16[8,48,4096]{2,1,0:T(8,128)(2,1)}), bf16[8,48,4096]{2,1,0:T(8,128)(2,1)}, u32[]{:S(2)}, u32[]{:S(2)}) %all-to-all-start) | async-done | bytes 3145760 | tf_op jit(solution)/shard_map/all_to_all | solution.py:98
  162.8 3.1 %fusion.42 = f32[1,1,64,64]{2,3,1,0:T(8,128)S(1)} fusion(bf16[384,64]{0,1:T(8,128)(2,1)S(1)} %fusion.21, bf16[384,4096]{1,0:T(8,128)(2,1)} %bitcast.8, bf16[4096,64]{0,1:T(8,128)(2,1)S(1)} %copy-done.1, f32[384]{0:T(512)S(1)} %mul.91, bf16[384]{0:T(512)(128)(2,1)S(1)} %and_convert_fusion.1), kind=kOutput, calls=%fused_computation.35 | convolution fusion | flops 204546048 | bytes 3737856 | tf_op jit(solution)/shard_map/ra,rib->iab/dot_general | solution.py:124
  166.2 1.4 collective-permute-start
  167.6 2.5 %collective-permute-done = f32[1,6144]{1,0:T(1,128)S(1)} collective-permute-done((f32[1,6144]{1,0:T(1,128)S(1)}, f32[1,6144]{1,0:T(1,128)S(1)}, u32[]{:S(2)}, u32[]{:S(2)}) %collective-permute-start) | collective-permute-done | bytes 24608 | tf_op jit(solution)/shard_map/ppermute | solution.py:13
  170.1 1.8 all-gather
  172.2 19.9 %psum.7 = f32[2,64]{1,0:T(2,128)} all-reduce(f32[2,64]{1,0:T(2,128)S(1)} %fusion.59), channel_id=1, replica_groups=mesh['group'=2,'expert'=8,'dp'=2] {'expert'}, use_global_device_ids=true, to_apply=%region_10.11 | all-reduce | flops 128 | bytes 1024 | tf_op jit(solution)/shard_map/psum | solution.py:137
  (49 shorter events, 3.1 us)
Async XLA Ops:
  0.0 5.1 %copy-start = (bf16[128,4096]{1,0:T(8,128)(2,1)S(1)}, bf16[128,4096]{1,0:T(8,128)(2,1)}, u32[]{:S(2)}) copy-start(bf16[128,4096]{1,0:T(8,128)(2,1)} %param.10) | copy-start | bytes 3145732
  7.8 78.1 %all-to-all-start.1 = ((bf16[8,48,4096]{2,1,0:T(8,128)(2,1)}), bf16[8,48,4096]{2,1,0:T(8,128)(2,1)}, u32[]{:S(2)}, u32[]{:S(2)}) async-start(bf16[8,48,4096]{2,1,0:T(8,128)(2,1)} %bitcast.159), calls=%async_computation.1 | async-start | bytes 6291456 | tf_op jit(solution)/shard_map/all_to_all | solution.py:91
  88.0 8.1 %copy-start.2 = (f32[2048,2]{0,1:T(2,128)S(1)}, f32[2048,2]{0,1:T(2,128)}, u32[]{:S(2)}) copy-start(f32[2048,2]{0,1:T(2,128)} %param.13) | copy-start | bytes 49156
  88.0 9.3 %copy-start.3 = (bf16[7168,64]{0,1:T(8,128)(2,1)S(1)}, bf16[7168,64]{0,1:T(8,128)(2,1)}, u32[]{:S(2)}) copy-start(bf16[7168,64]{0,1:T(8,128)(2,1)} %param.18) | copy-start | bytes 2752516
  88.0 74.9 %all-to-all-start = ((bf16[8,48,4096]{2,1,0:T(8,128)(2,1)}), bf16[8,48,4096]{2,1,0:T(8,128)(2,1)}, u32[]{:S(2)}, u32[]{:S(2)}) async-start(bf16[8,48,4096]{2,1,0:T(8,128)(2,1)} %bitcast.158), calls=%async_computation | async-start | bytes 6291456 | tf_op jit(solution)/shard_map/all_to_all | solution.py:98
  97.3 4.5 %copy-start.1 = (bf16[4096,64]{0,1:T(8,128)(2,1)S(1)}, bf16[4096,64]{0,1:T(8,128)(2,1)}, u32[]{:S(2)}) copy-start(bf16[4096,64]{0,1:T(8,128)(2,1)} %param.17) | copy-start | bytes 1572868
  115.7 56.2 %copy-start.4 = (bf16[64,6144]{1,0:T(8,128)(2,1)S(1)}, bf16[64,6144]{1,0:T(8,128)(2,1)}, u32[]{:S(2)}) copy-start(bf16[64,6144]{1,0:T(8,128)(2,1)} %param.19) | copy-start | bytes 2359300
  166.2 3.9 %collective-permute-start = (f32[1,6144]{1,0:T(1,128)S(1)}, f32[1,6144]{1,0:T(1,128)S(1)}, u32[]{:S(2)}, u32[]{:S(2)}) collective-permute-start(f32[1,6144]{1,0:T(1,128)S(1)} %constant_dynamic-slice_fusion), channel_id=1, source_target_pairs={{0,2},{2,0},{4,6},{6,4},{8,10},{10,8},{12,14},{14,12},{1,3},{3,1},... | collective-permute-start | bytes 73736 | tf_op jit(solution)/shard_map/ppermute | solution.py:13
where the time goes:
time: 193 us; the launch traced here: 192 us
  waiting for transfers between devices  119 us (62%)
  matrix products  24.1 us (12%)
  blocking collectives  21.8 us (11%)
  starting transfers between devices  13.5 us (7%)
  local copies, waits for them, and re-layouts  9.54 us (5%)
  other arithmetic  4.42 us (2%)
    all_to_all x1, waiting for transfers between devices, shards(): lax.all_to_all(jnp.repeat(buffer_tokens, HALVES, axis=0), 'expert', split...  69 us
    all_to_all x1, waiting for transfers between devices, shards(): lax.all_to_all(jnp.repeat(buffer_grads, HALVES, axis=0), 'expert', split_...  47.1 us
    psum x1, blocking collectives, shards(): return lax.psum(scores, 'expert')  19.9 us
    dot_general x3, matrix products, shards(): jnp.einsum('ra,rib->iab', projected, weighted, preferred_element_type=jnp...  13.9 us
    all_to_all x1, starting transfers between devices, shards(): lax.all_to_all(jnp.repeat(buffer_tokens, HALVES, axis=0), 'expert', split...  7.28 us
    all_to_all x1, starting transfers between devices, shards(): lax.all_to_all(jnp.repeat(buffer_grads, HALVES, axis=0), 'expert', split_...  4.75 us
    dot_general x1, matrix products, shards(): jnp.dot(values, factor, preferred_element_type=jnp.float32)  4.52 us
  transfers between devices with their start and end apart: 3, of which 3 were waited for; matrix products, arithmetic and copies ran while one was open for 13% of the time, Pallas kernels for 0%

commit v1 on v0

v1 whole, which is shorter than its diff:
```python
import functools

import jax
import jax.numpy as jnp
from jax import lax
from jax.experimental import pallas as pl
from jax.experimental.pallas import tpu as pltpu
from jax.sharding import PartitionSpec as P

HALVES = 2
LANES = 128
CHUNK = 512
TILE = 32
NT = (((1,), (1,)), ((), ()))
TN = (((0,), (0,)), ((), ()))
MESH = pl.DeviceIdType.MESH
F32 = jnp.float32
BF16 = jnp.bfloat16


def dot(a, b, dims=(((1,), (0,)), ((), ()))):
    return lax.dot_general(a, b, dims, preferred_element_type=F32)


def elementwise(gate, up, grad):
    gate = gate.astype(F32)
    up = up.astype(F32)
    grad = grad.astype(F32)
    sig = 0.5 * jnp.tanh(0.5 * gate) + 0.5
    silu = gate * sig
    slope = sig + silu * (1.0 - sig)
    return (
        (silu * up).astype(BF16),
        (grad * up * slope).astype(BF16),
        (grad * silu).astype(BF16),
    )


def kernel(
    peers, capacity, cap_rows,
    tokens, out_grad, routes, weights, gate, up, grad, model_t, hidden_t, val,
    out,
    tok_v, og_v, routes_v, weights_v, gate_v, up_v, grad_v, model_v, hidden_v, val_v,
    factor_v, act, acc, send_rows, recv_rows, part, part_send, part_recv, both, score_send, score_recv,
    load_sem, chunk_sem, row_send, row_recv, part_ssem, part_rsem, score_ssem, score_rsem,
):
    experts = peers // HALVES
    me = lax.axis_index("expert")
    core = lax.axis_index("dp")
    column = lax.rem(me, HALVES)
    partner = me + 1 - 2 * column
    tok_rows, k = tok_v.shape[0], model_v.shape[0]
    slot_rows, width = gate_v.shape
    chunks = width // CHUNK

    block = pl.ds(pl.multiple_of((me * 2 + core) * tok_rows, tok_rows), tok_rows)
    columns = pl.ds(pl.multiple_of(column * width, LANES), width)
    loads = [
        pltpu.make_async_copy(src, dst, load_sem.at[i])
        for i, (src, dst) in enumerate(
            (
                (routes.at[:, block], routes_v),
                (weights.at[:, block], weights_v),
                (model_t, model_v),
                (tokens, tok_v),
                (out_grad, og_v),
                (hidden_t.at[:, columns], hidden_v),
                (val, val_v),
            )
        )
    ]
    streams = [
        [
            pltpu.make_async_copy(
                src.at[0, :, pl.ds(c * CHUNK, CHUNK)],
                dst.at[:, pl.ds(c * CHUNK, CHUNK)],
                chunk_sem.at[i, c],
            )
            for i, (src, dst) in enumerate(((gate, gate_v), (up, up_v), (grad, grad_v)))
        ]
        for c in range(chunks)
    ]
    for copy in loads[:6]:
        copy.start()
    for group in streams:
        for copy in group:
            copy.start()
    loads[6].start()

    barrier = pltpu.get_barrier_semaphore()
    for d in range(1, peers):
        pl.semaphore_signal(
            barrier, inc=1, device_id={"expert": lax.rem(me + d, peers)}, device_id_type=MESH
        )
    pl.semaphore_signal(barrier, inc=1, device_id={"dp": 1 - core}, device_id_type=MESH)
    pl.semaphore_signal(
        barrier, inc=1, device_id={"expert": partner, "dp": 1 - core}, device_id_type=MESH
    )

    for copy in loads[:5]:
        copy.wait()
    proj = jnp.concatenate(
        [dot(tok_v[...], model_v[...], NT), dot(og_v[...], model_v[...], NT)], axis=1
    )
    lane = lax.broadcasted_iota(jnp.int32, (tok_rows, 2 * k), 1)
    high = proj.astype(BF16)
    low = jnp.where(lane < k, 0.0, proj - high.astype(F32)).astype(BF16)
    table = jnp.concatenate([high, low], axis=1)
    ids = lax.broadcasted_iota(jnp.int32, (experts, tok_rows), 0)
    first = routes_v[0:1, :] == ids
    second = routes_v[1:2, :] == ids
    named = jnp.where(first | second, 1.0, 0.0).astype(F32)
    row_weight = jnp.where(first, weights_v[0:1, :], jnp.where(second, weights_v[1:2, :], 0.0))
    square = (tok_rows, tok_rows)
    earlier = jnp.where(
        lax.broadcasted_iota(jnp.int32, square, 0) < lax.broadcasted_iota(jnp.int32, square, 1),
        1.0,
        0.0,
    ).astype(BF16)
    rank = dot(named.astype(BF16), earlier).astype(jnp.int32)
    slot = lax.broadcasted_iota(jnp.int32, (cap_rows, tok_rows), 0)
    slot_lane = lax.broadcasted_iota(jnp.int32, (cap_rows, 2 * k), 1)
    for e in range(experts):
        chosen = jnp.where(
            (rank[e : e + 1, :] == slot) & (slot < capacity), named[e : e + 1, :], 0.0
        )
        slot_weight = jnp.sum(chosen * row_weight[e : e + 1, :], axis=1, keepdims=True)
        picked = dot(chosen.astype(BF16), table)
        rows = picked[:, : 2 * k] + picked[:, 2 * k :]
        send_rows[e] = jnp.where(slot_lane < k, rows, rows * slot_weight).astype(BF16)
    pl.semaphore_wait(barrier, peers + 1)
    row_copies = []
    for d in range(1, peers):
        target = lax.rem(me + d, peers)
        copy = pltpu.make_async_remote_copy(
            src_ref=send_rows.at[target // HALVES],
            dst_ref=recv_rows.at[me],
            send_sem=row_send.at[d - 1],
            recv_sem=row_recv.at[d - 1],
            device_id={"expert": target},
            device_id_type=MESH,
        )
        copy.start()
        row_copies.append(copy)
    recv_rows[me] = send_rows[me // HALVES]

    loads[5].wait()
    shape = (k, k)
    to, source = (lax.broadcasted_iota(jnp.int32, shape, axis) for axis in (0, 1))
    order = jnp.where(source == jnp.where(to < k // 2, 2 * to, 2 * to - k + 1), 1.0, 0.0)
    order = order.astype(BF16)
    for c in range(chunks):
        here = pl.ds(c * CHUNK, CHUNK)
        factor_v[:, here] = dot(order, hidden_v[:, here]).astype(BF16)

    def multiply(c):
        here = pl.ds(c * CHUNK, CHUNK)
        value = dot(act[c % 2], factor_v[:, here], NT)
        if c == 0:
            acc[...] = value
        else:
            acc[...] += value

    for c in range(chunks):
        for copy in streams[c]:
            copy.wait()
        here = pl.ds(c * CHUNK, CHUNK)
        for t in range(slot_rows // TILE):
            rows = pl.ds(t * TILE, TILE)
            values = elementwise(gate_v[rows, here], up_v[rows, here], grad_v[rows, here])
            for i, value in enumerate(values):
                act[c % 2, pl.ds(i * slot_rows + t * TILE, TILE), :] = value
        if c > 0:
            multiply(c - 1)
    multiply(chunks - 1)

    for copy in row_copies:
        copy.wait()
    pairs = recv_rows[...].reshape(peers * cap_rows, 2 * k)
    if cap_rows != capacity:
        grid = (slot_rows, peers * cap_rows)
        row, col = (lax.broadcasted_iota(jnp.int32, grid, axis) for axis in (0, 1))
        spot = (row // capacity) * cap_rows + row % capacity
        pairs = dot(jnp.where(col == spot, 1.0, 0.0).astype(BF16), pairs).astype(BF16)
    half = k // 2
    half_lane = lax.broadcasted_iota(jnp.int32, (half, 2 * k), 1)
    blocks = []
    for i in range(3):
        sketch = acc[pl.ds(i * slot_rows, slot_rows), :].astype(BF16)
        outer = dot(sketch, pairs, TN)
        even, odd = outer[:half], outer[half:]
        if i == 0:
            even = pltpu.roll(even, k, 1)
        else:
            odd = pltpu.roll(odd, k, 1)
        blocks.append(jnp.where(half_lane < k, even, odd))
    whole = jnp.concatenate(blocks, axis=0)
    part_rows = whole.shape[0] // HALVES
    for c in range(HALVES):
        piece = whole[c * part_rows : (c + 1) * part_rows]
        part[c] = piece
        part_send[c] = piece.astype(BF16)
    part_copies = []
    for i, (which, device) in enumerate(
        (
            (1 - column, {"expert": partner}),
            (1 - column, {"expert": partner, "dp": 1 - core}),
            (column, {"dp": 1 - core}),
        )
    ):
        copy = pltpu.make_async_remote_copy(
            src_ref=part_send.at[which],
            dst_ref=part_recv.at[i],
            send_sem=part_ssem.at[i],
            recv_sem=part_rsem.at[i],
            device_id=device,
            device_id_type=MESH,
        )
        copy.start()
        part_copies.append(copy)
    loads[6].wait()
    for copy in part_copies:
        copy.wait()
    own = part[column] + part_recv[0].astype(F32)
    other = part_recv[1].astype(F32) + part_recv[2].astype(F32)
    both[0] = jnp.where(core == 0, own, other)
    both[1] = jnp.where(core == 0, other, own)
    totals = [jnp.zeros((val_v.shape[0], LANES), F32) for _ in range(2)]
    for i in range(part_rows):
        values = val_v[:, pl.ds(i * LANES, LANES)].astype(F32)
        for n in range(2):
            totals[n] = totals[n] + values * both[n, pl.ds(i, 1), :]
    scores = jnp.sum(jnp.concatenate(totals, axis=0).T, axis=0, keepdims=True)
    score_send[...] = jnp.broadcast_to(scores, score_send.shape)
    score_copies = []
    for d in range(1, peers):
        copy = pltpu.make_async_remote_copy(
            src_ref=score_send,
            dst_ref=score_recv.at[d - 1],
            send_sem=score_ssem.at[d - 1],
            recv_sem=score_rsem.at[d - 1],
            device_id={"expert": lax.rem(me + d, peers)},
            device_id_type=MESH,
        )
        copy.start()
        score_copies.append(copy)
    for copy in score_copies:
        copy.wait()
    total = score_send[...]
    for d in range(1, peers):
        total = total + score_recv[d - 1]
    count = val_v.shape[0]
    out[0:1, :] = total[0:1, :count]
    out[1:2, :] = total[0:1, count : 2 * count]


def shards(
    tokens, out_grad, routes, route_weight, gate_pre, up_pre, hid_grad, proj_model, proj_hidden, val_sketch
):
    peers = lax.axis_size("expert")
    tok_rows, model = tokens.shape
    _, slot_rows, width = gate_pre.shape
    k = proj_model.shape[1]
    capacity = slot_rows // peers
    cap_rows = -(-capacity // 16) * 16
    val_rows, entries = val_sketch.shape
    part_rows = entries // LANES
    chunks = width // CHUNK
    experts = peers // HALVES
    vmem, dma = pltpu.VMEM, pltpu.SemaphoreType.DMA
    return pl.pallas_call(
        functools.partial(kernel, peers, capacity, cap_rows),
        out_shape=jax.ShapeDtypeStruct((2, val_rows), F32),
        in_specs=[pl.BlockSpec(memory_space=pltpu.HBM)] * 10,
        out_specs=pl.BlockSpec(memory_space=pltpu.VMEM),
        scratch_shapes=[
            vmem((tok_rows, model), BF16),
            vmem((tok_rows, model), BF16),
            vmem((2, tok_rows), jnp.int32),
            vmem((2, tok_rows), F32),
            vmem((slot_rows, width), BF16),
            vmem((slot_rows, width), BF16),
            vmem((slot_rows, width), BF16),
            vmem((k, model), BF16),
            vmem((k, width), BF16),
            vmem((val_rows, entries), BF16),
            vmem((k, width), BF16),
            vmem((2, 3 * slot_rows, CHUNK), BF16),
            vmem((3 * slot_rows, k), F32),
            vmem((experts, cap_rows, 2 * k), BF16),
            vmem((peers, cap_rows, 2 * k), BF16),
            vmem((HALVES, part_rows, LANES), F32),
            vmem((HALVES, part_rows, LANES), BF16),
            vmem((3, part_rows, LANES), BF16),
            vmem((2, part_rows, LANES), F32),
            vmem((8, LANES), F32),
            vmem((peers - 1, 8, LANES), F32),
            dma((7,)),
            dma((3, chunks)),
            dma((peers - 1,)),
            dma((peers - 1,)),
            dma((3,)),
            dma((3,)),
            dma((peers - 1,)),
            dma((peers - 1,)),
        ],
        compiler_params=pltpu.CompilerParams(
            collective_id=0, has_side_effects=True, vmem_limit_bytes=56 * 2**20
        ),
        cost_estimate=pl.CostEstimate(
            flops=2 * 3 * slot_rows * width * k, bytes_accessed=12 * 2**20, transcendentals=slot_rows * width
        ),
    )(
        tokens, out_grad, routes.T, route_weight.T, gate_pre, up_pre, hid_grad,
        proj_model.T, proj_hidden.T, val_sketch,
    )


def solution(mesh):
    return jax.shard_map(
        shards,
        mesh=mesh,
        in_specs=(
            P(("group", "expert", "dp"), None),
            P(("group", "expert", "dp"), None),
            P("group", None),
            P("group", None),
            P("expert", ("group", "dp"), None),
            P("expert", ("group", "dp"), None),
            P("expert", ("group", "dp"), None),
            P(),
            P(),
            P("dp", "expert"),
        ),
        out_specs=P("group", "dp"),
        check_vma=False,
    )
```

time: 193 us -> 24.9 us (0.13)
  waiting for transfers between devices: 119 us -> 0 us
  matrix products: 24.1 us -> 0 us
  Pallas kernels: 0 us -> 23.5 us
  blocking collectives: 21.8 us -> 0 us
  starting transfers between devices: 13.5 us -> 0 us
  local copies, waits for them, and re-layouts: 9.54 us -> 1.24 us
  other arithmetic: 4.42 us -> 0 us
    all_to_all x2 -> x0, waiting for transfers between devices: 116 us -> none  [the longest x1 69 us: shards(): lax.all_to_all(jnp.repeat(buffer_tokens, HALVES, axis=0), 'expert', split...]
    dot_general x8 -> x0, matrix products: 24.1 us -> none  [the longest x3 13.9 us: shards(): jnp.einsum('ra,rib->iab', projected, weighted, preferred_element_type=jnp...]
    pallas_call x0 -> x1, Pallas kernels: none -> 23.5 us  [shards(): pl.pallas_call(functools.partial(kernel, peers, capacity, cap_rows), out_...]
    psum x1 -> x0, blocking collectives: 19.9 us -> none  [shards(): return lax.psum(scores, 'expert')]
    all_to_all x2 -> x0, starting transfers between devices: 12 us -> none  [the longest x1 7.28 us: shards(): lax.all_to_all(jnp.repeat(buffer_tokens, HALVES, axis=0), 'expert', split...]
    broadcast_in_dim x2 -> x0, local copies, waits for them, and re-layouts: 4.15 us -> none  [the longest x1 2.08 us: shards(): jnp.repeat(buffer_tokens, HALVES, axis=0)]
    another operation x5 -> x0, other arithmetic: 3.56 us -> none
    ppermute x1 -> x0, waiting for transfers between devices: 2.46 us -> none  [partner_2(): return lax.ppermute(value, axis, pairs)]
  transfers between devices with their start and end apart: 3 -> 0, of which waited for: 3 -> 0; matrix products, arithmetic and copies ran while one was open for 13% -> 0% of each run, Pallas kernels for 0% -> 0%
where the time goes in v1:
time: 24.9 us; the launch traced here: 24.8 us
  Pallas kernels  23.5 us (94%)
  local copies, waits for them, and re-layouts  1.24 us (5%)
    pallas_call x1, Pallas kernels, shards(): pl.pallas_call(functools.partial(kernel, peers, capacity, cap_rows), out_...  23.5 us
    unnamed x1, local copies, waits for them, and re-layouts  1.24 us

profile of v1, /device:TPU:0, one launch (start us, length us, event | category | flops | bytes accessed | tf_op | source)
XLA Modules:
  0.0 24.8 jit_solution(11727179198994343633)
XLA Ops:
  0.0 23.5 %shard_map.100 = f32[2,64]{1,0:T(2,128)} custom-call(bf16[128,4096]{1,0:T(8,128)(2,1)} %tokens.1, bf16[128,4096]{1,0:T(8,128)(2,1)} %out_grad.1, s32[2,2048]{1,0:T(2,128)} %bitcast.6, f32[2,2048]{1,0:T(2,128)} %bitcast.7, bf16[1,384,3584]{2,1,0:T(8,128)(2,1)} %gate.1, bf16[1,384,3584]{2,1,0:T(8,128)(2,1)} %up.1, bf16[1,384,3584]{2,1,0:T(8,128)(2,1)} %grad.1, ...), custom_call_target="tpu_custom_call" | custom-call | flops 528482304 | bytes 12582912 | tf_op jit(solution)/shard_map/pallas_call | solution.py:271
  23.5 1.2 %copy.12 = f32[2,64]{1,0:T(2,128)} copy(f32[2,64]{1,0:T(2,128)} %shard_map.100) | data formatting | bytes 1024

commit v2 on v1

--- a/solution.py
+++ b/solution.py
@@ -10,7 +10,7 @@
 HALVES = 2
 LANES = 128
 CHUNK = 512
-TILE = 32
+TILE = 128
 NT = (((1,), (1,)), ((), ()))
 TN = (((0,), (0,)), ((), ()))
 MESH = pl.DeviceIdType.MESH
@@ -24,11 +24,11 @@
 
 def elementwise(gate, up, grad):
     gate = gate.astype(F32)
-    up = up.astype(F32)
-    grad = grad.astype(F32)
     sig = 0.5 * jnp.tanh(0.5 * gate) + 0.5
     silu = gate * sig
     slope = sig + silu * (1.0 - sig)
+    up = up.astype(F32)
+    grad = grad.astype(F32)
     return (
         (silu * up).astype(BF16),
         (grad * up * slope).astype(BF16),
@@ -41,7 +41,7 @@
     tokens, out_grad, routes, weights, gate, up, grad, model_t, hidden_t, val,
     out,
     tok_v, og_v, routes_v, weights_v, gate_v, up_v, grad_v, model_v, hidden_v, val_v,
-    factor_v, act, acc, send_rows, recv_rows, part, part_send, part_recv, both, score_send, score_recv,
+    factor_v, acc, send_rows, recv_rows, part, part_send, part_recv, both, score_send, score_recv,
     load_sem, chunk_sem, row_send, row_recv, part_ssem, part_rsem, score_ssem, score_rsem,
 ):
     experts = peers // HALVES
@@ -151,15 +151,7 @@
     order = order.astype(BF16)
     for c in range(chunks):
         here = pl.ds(c * CHUNK, CHUNK)
-        factor_v[:, here] = dot(order, hidden_v[:, here]).astype(BF16)
-
-    def multiply(c):
-        here = pl.ds(c * CHUNK, CHUNK)
-        value = dot(act[c % 2], factor_v[:, here], NT)
-        if c == 0:
-            acc[...] = value
-        else:
-            acc[...] += value
+        factor_v[here, :] = dot(hidden_v[:, here], order, (((0,), (1,)), ((), ()))).astype(BF16)
 
     for c in range(chunks):
         for copy in streams[c]:
@@ -168,11 +160,11 @@
         for t in range(slot_rows // TILE):
             rows = pl.ds(t * TILE, TILE)
             values = elementwise(gate_v[rows, here], up_v[rows, here], grad_v[rows, here])
-            for i, value in enumerate(values):
-                act[c % 2, pl.ds(i * slot_rows + t * TILE, TILE), :] = value
-        if c > 0:
-            multiply(c - 1)
-    multiply(chunks - 1)
+            product = dot(jnp.concatenate(values, axis=0), factor_v[here, :])
+            for i in range(3):
+                piece = product[i * TILE : (i + 1) * TILE]
+                spot = pl.ds(i * slot_rows + t * TILE, TILE)
+                acc[spot, :] = piece if c == 0 else acc[spot, :] + piece
 
     for copy in row_copies:
         copy.wait()
@@ -284,8 +276,7 @@
             vmem((k, model), BF16),
             vmem((k, width), BF16),
             vmem((val_rows, entries), BF16),
-            vmem((k, width), BF16),
-            vmem((2, 3 * slot_rows, CHUNK), BF16),
+            vmem((width, k), BF16),
             vmem((3 * slot_rows, k), F32),
             vmem((experts, cap_rows, 2 * k), BF16),
             vmem((peers, cap_rows, 2 * k), BF16),

time: 24.9 us -> 23.1 us (0.928)
  Pallas kernels: 23.5 us -> 21.7 us
    pallas_call x1, Pallas kernels: 23.5 us -> 21.7 us  [shards(): pl.pallas_call(functools.partial(kernel, peers, capacity, cap_rows), out_...]
where the time goes in v2:
time: 23.1 us; the launch traced here: 22.9 us
  Pallas kernels  21.7 us (94%)
  local copies, waits for them, and re-layouts  1.24 us (5%)
    pallas_call x1, Pallas kernels, shards(): pl.pallas_call(functools.partial(kernel, peers, capacity, cap_rows), out_...  21.7 us
    unnamed x1, local copies, waits for them, and re-layouts  1.24 us

profile of v2, /device:TPU:0, one launch (start us, length us, event | category | flops | bytes accessed | tf_op | source)
XLA Modules:
  0.0 22.9 jit_solution(7641651060628758375)
XLA Ops:
  0.0 21.7 %shard_map.100 = f32[2,64]{1,0:T(2,128)} custom-call(bf16[128,4096]{1,0:T(8,128)(2,1)} %tokens.1, bf16[128,4096]{1,0:T(8,128)(2,1)} %out_grad.1, s32[2,2048]{1,0:T(2,128)} %bitcast.6, f32[2,2048]{1,0:T(2,128)} %bitcast.7, bf16[1,384,3584]{2,1,0:T(8,128)(2,1)} %gate.1, bf16[1,384,3584]{2,1,0:T(8,128)(2,1)} %up.1, bf16[1,384,3584]{2,1,0:T(8,128)(2,1)} %grad.1, ...), custom_call_target="tpu_custom_call" | custom-call | flops 528482304 | bytes 12582912 | tf_op jit(solution)/shard_map/pallas_call | solution.py:263
  21.7 1.2 %copy.12 = f32[2,64]{1,0:T(2,128)} copy(f32[2,64]{1,0:T(2,128)} %shard_map.100) | data formatting | bytes 1024
